TPU v7x, 32 devices: a whole 2x2x4 slice. The times are simulated.
32 devices in a mesh: dp: 8 (over y, x, core), space: 4 (over z).
Axes of the slice: x: 2, y: 2, z: 4, core: 2. Of those that a mesh axis runs over, the one named last changes fastest.
Arguments:
- images: bfloat16 [8, 16, 128, 1024], P('dp', 'space'), may hold values from -18 to 18
- teacher: bfloat16 [8, 16, 128, 1024], P('dp', 'space'), may hold values from 0 to 400
- w_reduce: bfloat16 [1024, 256], replicated, may hold values from -0.1875 to 0.1875
- w_spatial: bfloat16 [3, 3, 256, 256], replicated, may hold values from -0.125 to 0.125
- w_expand: bfloat16 [256, 1024], replicated, may hold values from -0.375 to 0.375
- partners: int32 [2, 8], replicated, may hold values from 0 to 7, as said below
Outputs:
- distill_loss: float32 [], replicated
- grad_images: bfloat16 [8, 16, 128, 1024], P('dp', 'space')
- grad_reduce: float32 [8, 1024, 256], P('dp', 'space')
- grad_spatial: float32 [8, 3, 3, 256, 256], P('dp', None, None, None, 'space')
- grad_expand: float32 [8, 256, 1024], P('dp', None, 'space')
Inputs may be any that keep to these rules, and one draw needn't show every extreme that they name: partners[r, i] = i XOR m_r for a round value m_r of 1 to 7, the m_r distinct over rounds; so each round pairs the images and partners[r, partners[r, i]] = i.
All inputs are finite; a program needn't handle non-finite values.
Results may differ from a plain program's by a relative error of at most 0.019.
The roundings to bfloat16 on the way count: a program that leaves them out, or rounds other values in their place, can miss the bound.
Values may be sent and summed in bfloat16 or wider, within the bound.
A program may use at most 64 MiB of HBM per device.

v0:
```python
import jax
import jax.numpy as jnp
from jax import lax
from jax.sharding import PartitionSpec as P


def extended(shard, sides, width):
    for axis, dim in sides:
        peers, length = (lax.axis_size(axis), shard.shape[dim])
        up = [(i, (i + 1) % peers) for i in range(peers - 1)]
        down = [(j, i) for i, j in up]
        last = lax.slice_in_dim(shard, length - width, length, axis=dim)
        initial = lax.slice_in_dim(shard, 0, width, axis=dim)
        before = lax.ppermute(last, axis, up)
        after = lax.ppermute(initial, axis, down)
        shard = jnp.concatenate([before, shard, after], axis=dim)
    return shard


def gram_table(features, partners):
    columns = [jnp.einsum("ie,ie->i", features, features, preferred_element_type=jnp.float32)]
    for round_index in range(partners.shape[0]):
        columns.append(
            jnp.einsum(
                "ie,ie->i",
                features,
                features[partners[round_index]],
                preferred_element_type=jnp.float32,
            )
        )
    return jnp.stack(columns, axis=1)


def slices_route(student_img, teacher, partners, elems_total):
    student_cut, teacher_cut = (
        lax.all_to_all(student_img, "dp", split_axis=2, concat_axis=0, tiled=True),
        lax.all_to_all(teacher, "dp", split_axis=2, concat_axis=0, tiled=True),
    )
    image_count = student_cut.shape[0]
    student_rows = student_cut.reshape(image_count, -1)
    teacher_rows = teacher_cut.reshape(image_count, -1)
    v_student, v_teacher = lax.psum(
        (gram_table(student_rows, partners), gram_table(teacher_rows, partners)), ("dp", "space")
    )
    nu_student = jnp.sqrt(jnp.sum(v_student * v_student, axis=1, keepdims=True) + 1e-06)
    nu_teacher = jnp.sqrt(jnp.sum(v_teacher * v_teacher, axis=1, keepdims=True) + 1e-06)
    n_student = v_student / nu_student
    n_teacher = v_teacher / nu_teacher
    diff = n_student - n_teacher
    distill_loss = jnp.sum(diff * diff)
    err_table = 2.0 * diff
    coefs = (
        err_table - jnp.sum(err_table * n_student, axis=1, keepdims=True) * n_student
    ) / nu_student
    summed = 2.0 * coefs[:, 0:1] * student_rows.astype(jnp.float32)
    for round_index in range(partners.shape[0]):
        partner = partners[round_index]
        weight = coefs[:, round_index + 1] + coefs[partner, round_index + 1]
        summed = summed + weight[:, None] * student_rows[partner].astype(jnp.float32)
    grad_cut = (elems_total * summed).astype(jnp.bfloat16).reshape(student_cut.shape)
    returned = lax.all_to_all(grad_cut, "dp", split_axis=0, concat_axis=2, tiled=True)
    return (distill_loss, returned.reshape(-1, returned.shape[-1]))


def body(images, teacher, w_reduce, w_spatial, w_expand, partners):
    _, row_count, col_count, channels = images.shape
    hidden = w_reduce.shape[1]
    elems_total = row_count * lax.axis_size("space") * col_count * channels
    flat_x = images.reshape(-1, channels)
    h_one = jax.nn.relu(jnp.dot(flat_x, w_reduce, preferred_element_type=jnp.float32)).astype(
        jnp.bfloat16
    )
    h_one_img = h_one.reshape(1, row_count, col_count, hidden)
    pad_one = extended(h_one_img, (("space", 1),), 1)
    pad_one = jnp.pad(pad_one, ((0, 0), (0, 0), (1, 1), (0, 0)))
    patches = jnp.concatenate(
        [
            pad_one[:, row_step : row_step + row_count, col_step : col_step + col_count, :]
            for row_step in range(3)
            for col_step in range(3)
        ],
        axis=-1,
    ).reshape(-1, 9 * hidden)
    h_two = jax.nn.relu(
        jnp.dot(patches, w_spatial.reshape(9 * hidden, hidden), preferred_element_type=jnp.float32)
    ).astype(jnp.bfloat16)
    pre_act = jnp.dot(h_two, w_expand, preferred_element_type=jnp.float32) + flat_x.astype(
        jnp.float32
    )
    student = jax.nn.relu(pre_act).astype(jnp.bfloat16)
    student_img = student.reshape(images.shape)
    distill_loss, grad_student = slices_route(student_img, teacher, partners, elems_total)
    g_pre = jnp.where(student > 0, grad_student, jnp.zeros_like(grad_student))
    local_expand = jnp.dot(h_two.T, g_pre, preferred_element_type=jnp.float32)
    back_two = jnp.dot(g_pre, w_expand.T, preferred_element_type=jnp.float32)
    g_two = jnp.where(h_two > 0, back_two, 0.0).astype(jnp.bfloat16)
    local_spatial = jnp.dot(patches.T, g_two, preferred_element_type=jnp.float32).reshape(
        3, 3, hidden, hidden
    )
    pad_grad = extended(g_two.reshape(1, row_count, col_count, hidden), (("space", 1),), 1)
    pad_grad = jnp.pad(pad_grad, ((0, 0), (0, 0), (1, 1), (0, 0)))
    grad_patches = jnp.concatenate(
        [
            pad_grad[
                :,
                2 - row_step : 2 - row_step + row_count,
                2 - col_step : 2 - col_step + col_count,
                :,
            ]
            for row_step in range(3)
            for col_step in range(3)
        ],
        axis=-1,
    ).reshape(-1, 9 * hidden)
    w_back = jnp.concatenate(
        [w_spatial[row_step, col_step].T for row_step in range(3) for col_step in range(3)], axis=0
    )
    back_one = jnp.dot(grad_patches, w_back, preferred_element_type=jnp.float32)
    g_one = jnp.where(h_one > 0, back_one, 0.0).astype(jnp.bfloat16)
    local_reduce = jnp.dot(flat_x.T, g_one, preferred_element_type=jnp.float32)
    grad_images = (
        (g_pre.astype(jnp.float32) + jnp.dot(g_one, w_reduce.T, preferred_element_type=jnp.float32))
        .astype(jnp.bfloat16)
        .reshape(images.shape)
    )
    grad_spatial = lax.psum_scatter(
        local_spatial[None].astype(jnp.bfloat16), "space", scatter_dimension=4, tiled=True
    ).astype(jnp.float32)
    grad_reduce, grad_expand = (
        lax.psum_scatter(
            local_reduce[None].astype(jnp.bfloat16), "space", scatter_dimension=1, tiled=True
        ).astype(jnp.float32),
        lax.psum_scatter(
            local_expand[None].astype(jnp.bfloat16), "space", scatter_dimension=2, tiled=True
        ).astype(jnp.float32),
    )
    return (distill_loss, grad_images, grad_reduce, grad_spatial, grad_expand)


def solution(mesh):
    return jax.shard_map(
        body,
        mesh=mesh,
        in_specs=(P("dp", "space", None, None), P("dp", "space", None, None), P(), P(), P(), P()),
        out_specs=(
            P(),
            P("dp", "space", None, None),
            P("dp", "space", None),
            P("dp", None, None, None, "space"),
            P("dp", None, "space"),
        ),
        check_vma=False,
    )
```

profile of v0, /device:TPU:11, one launch (start us, length us, event | category | flops | bytes accessed | tf_op | source)
XLA Modules:
  0.0 257.7 jit_solution(9031558274081741423)
XLA Ops:
  7.2 3.1 %copy.27 = bf16[1,4,128,1024]{3,1,0,2:T(4,128)(2,1)} copy(bf16[1,4,128,1024]{3,2,1,0:T(8,128)(2,1)} %param.7) | data formatting | bytes 2097152 | tf_op args[1]
  10.4 4.7 %all-to-all-start.1 = ((bf16[1,4,128,1024]{3,1,0,2:T(4,128)(2,1)}), bf16[1,4,128,1024]{3,1,0,2:T(4,128)(2,1)S(1)}, u32[]{:S(2)}, u32[]{:S(2)}) async-start(bf16[1,4,128,1024]{3,1,0,2:T(4,128)(2,1)} %copy.27), calls=%async_computation.1 | async-start | bytes 2097152 | tf_op jit(solution)/shard_map/all_to_all | solution.py:37
  15.5 2.1 collective-permute-start.1
  17.6 3.2 %collective-permute-start = (bf16[1,1,128,256]{3,2,1,0:T(8,128)(2,1)S(1)}, bf16[1,1,128,256]{3,2,1,0:T(8,128)(2,1)S(1)}, u32[]{:S(2)}, u32[]{:S(2)}) collective-permute-start(bf16[1,1,128,256]{3,2,1,0:T(8,128)(2,1)S(1)} %get-tuple-element.49), channel_id=1, source_target_pairs={{0,1},{1,2},{2,3},{4,5},{5,6},{6,7},{8,9},{9,10},{10,11},{12,13},{... | collective-permute-start | bytes 196616 | tf_op jit(solution)/shard_map/ppermute | solution.py:14
  20.8 0.7 bitcast_dynamic-update-slice_fusion.8
  22.2 0.7 collective-permute-done
  23.5 0.8 fusion.14
  25.4 1.1 copy-done.1
  26.5 1.8 copy.25
  28.9 5.1 %all-to-all-start = ((bf16[1,4,128,1024]{3,1,0,2:T(4,128)(2,1)}), bf16[1,4,128,1024]{3,1,0,2:T(4,128)(2,1)S(1)}, u32[]{:S(2)}, u32[]{:S(2)}) async-start(bf16[1,4,128,1024]{3,1,0,2:T(4,128)(2,1)} %copy.25), calls=%async_computation | async-start | bytes 2097152 | tf_op jit(solution)/shard_map/all_to_all | solution.py:36
  33.9 1.6 bitcast_dynamic-update-slice_fusion.6
  35.5 1.6 bitcast_dynamic-update-slice_fusion.5
  37.1 1.8 copy.28
  38.9 2.2 gather_fusion.2
  41.1 2.2 gather_fusion.3
  43.4 2.3 fusion.3
  45.7 2.1 all-to-all-done
  47.8 1.3 copy.73
  49.1 1.7 reshape.167
  50.8 1.2 gather_fusion
  52.0 2.2 gather_fusion.1
  54.3 2.0 fusion
  56.2 1.6 bitcast_dynamic-update-slice_fusion.4
  57.8 39.4 %all-reduce.5 = (f32[8,3]{0,1:T(4,128)S(1)}, f32[8,3]{0,1:T(4,128)S(1)}) all-reduce(f32[8,3]{0,1:T(4,128)S(1)} %pad_maximum_fusion.5, f32[8,3]{0,1:T(4,128)S(1)} %pad_maximum_fusion.4), channel_id=1, replica_groups=mesh['dp'=8,'space'=4] {'dp','space'}, use_global_device_ids=true, to_apply=%region_2.3 | all-reduce | flops 48 | bytes 384 | tf_op jit(solution)/shard_map/psum | solution.py:42
  97.3 2.8 %convert.57 = f32[8,4,16,1024]{3,0,2,1:T(8,128)} convert(bf16[8,4,16,1024]{3,0,2,1:T(8,128)(2,1)} %bitcast.160) | non-fusion elementwise | flops 524288 | bytes 3145728 | tf_op jit(solution)/shard_map/convert_element_type | solution.py:59
  100.1 1.6 convert.58
  103.7 6.0 %fusion.9 = bf16[8,4,16,1024]{3,2,1,0:T(8,128)(2,1)} fusion(f32[8,4,16,1024]{3,0,2,1:T(8,128)} %convert.57, f32[8,4,16,1024]{3,0,2,1:T(8,128)} %convert.58, f32[8]{0:T(128)S(1)} %get-tuple-element.52, f32[8]{0:T(128)S(1)} %get-tuple-element.53, f32[8]{0:T(128)S(1)} %get-tuple-element.51, bf16[1,4,8,16,1024]{4,1,3,2,0:T(4,128)(2,1)S(1)} %bitcast.164), kind=kLoop, calls=%fused_computation.22 | loop fusion | flops 4194304 | bytes 6291552 | tf_op jit(solution)/shard_map/convert_element_type | solution.py:60
  109.7 5.4 %all-to-all-start.2 = ((bf16[8,4,16,1024]{3,2,1,0:T(8,128)(2,1)}), bf16[8,4,16,1024]{3,2,1,0:T(8,128)(2,1)S(1)}, u32[]{:S(2)}, u32[]{:S(2)}) async-start(bf16[8,4,16,1024]{3,2,1,0:T(8,128)(2,1)} %fusion.9), calls=%async_computation.2 | async-start | bytes 2097152 | tf_op jit(solution)/shard_map/all_to_all | solution.py:61
  115.0 1.7 bitcast_dynamic-update-slice_fusion.3
  116.7 1.6 bitcast_dynamic-update-slice_fusion.2
  118.3 1.6 bitcast_dynamic-update-slice_fusion.1
  119.9 1.6 bitcast_dynamic-update-slice_fusion
  121.5 7.4 %all-to-all-done.2 = bf16[8,4,16,1024]{3,2,1,0:T(8,128)(2,1)S(1)} async-done(((bf16[8,4,16,1024]{3,2,1,0:T(8,128)(2,1)}), bf16[8,4,16,1024]{3,2,1,0:T(8,128)(2,1)S(1)}, u32[]{:S(2)}, u32[]{:S(2)}) %all-to-all-start.2) | async-done | bytes 1048608 | tf_op jit(solution)/shard_map/all_to_all | solution.py:61
  129.7 2.1 collective-permute-start.3
  131.8 3.1 %collective-permute-start.2 = (bf16[1,1,128,256]{3,2,1,0:T(8,128)(2,1)S(1)}, bf16[1,1,128,256]{3,2,1,0:T(8,128)(2,1)S(1)}, u32[]{:S(2)}, u32[]{:S(2)}) collective-permute-start(bf16[1,1,128,256]{3,2,1,0:T(8,128)(2,1)S(1)} %get-tuple-element.45), channel_id=1, source_target_pairs={{0,1},{1,2},{2,3},{4,5},{5,6},{6,7},{8,9},{9,10},{10,11},{12,13},{... | collective-permute-start | bytes 196616 | tf_op jit(solution)/shard_map/ppermute | solution.py:14
  135.0 1.3 fusion.12
  137.4 2.2 fusion.15
  139.6 1.3 fusion.11
  140.9 4.3 %copy.32 = bf16[2304,512]{1,0:T(8,128)(2,1)} copy(bf16[2304,512]{0,1:T(8,128)(2,1)} %bitcast.177) | data formatting | bytes 4718592 | tf_op jit(solution)/shard_map/dot_general | solution.py:97
  145.2 2.5 fusion.10
  147.7 2.2 copy.33
  151.2 2.5 add_convert_fusion
  153.7 1.6 convert_element_type.106
  155.3 21.1 %reduce-scatter.3.cloned.1.call-done = bf16[1,256,256]{1,2,0:T(8,128)(2,1)} async-done(((bf16[1,1024,256]{1,2,0:T(8,128)(2,1)}), bf16[1,256,256]{1,2,0:T(8,128)(2,1)}) %reduce-scatter.3.cloned.1.call-update) | async-done | bytes 131088 | tf_op jit(solution)/shard_map/reduce_scatter | solution.py:130
  176.4 1.7 copy.34
  178.1 71.0 %all-reduce.8.cloned.1.call-done = bf16[1,3,3,256,256]{3,2,1,0,4:T(4,128)(2,1)} async-done(((bf16[1,3,3,256,256]{3,2,1,0,4:T(4,128)(2,1)}), bf16[1,3,3,256,256]{3,2,1,0,4:T(4,128)(2,1)}) %all-reduce.8.cloned.1.call-update) | async-done | bytes 1179664
  249.1 1.1 dynamic-slice_convert_fusion
  250.2 0.9 copy.35
  (82 shorter events, 7.9 us)
Async XLA Ops:
  7.2 17.8 %copy-start = (bf16[256,1024]{1,0:T(8,128)(2,1)S(1)}, bf16[256,1024]{1,0:T(8,128)(2,1)}, u32[]{:S(2)}) copy-start(bf16[256,1024]{1,0:T(8,128)(2,1)} %param.10) | copy-start | bytes 1572868
  7.2 7.9 %copy-start.6 = (bf16[1,4,128,1024]{3,2,1,0:T(8,128)(2,1)S(1)}, bf16[1,4,128,1024]{3,2,1,0:T(8,128)(2,1)}, u32[]{:S(2)}) copy-start(bf16[1,4,128,1024]{3,2,1,0:T(8,128)(2,1)} %param.6) | copy-start | bytes 3145732
  7.2 7.9 %copy-start.10 = (bf16[1024,256]{1,0:T(8,128)(2,1)S(1)}, bf16[1024,256]{1,0:T(8,128)(2,1)}, u32[]{:S(2)}) copy-start(bf16[1024,256]{1,0:T(8,128)(2,1)} %param.8) | copy-start | bytes 1572868
  10.4 11.8 %copy-start.11 = (s32[2,8]{1,0:T(2,128)S(1)}, s32[2,8]{1,0:T(2,128)}, u32[]{:S(2)}) copy-start(s32[2,8]{1,0:T(2,128)} %param.11) | copy-start | bytes 196
  10.4 18.5 %all-to-all-start.1 = ((bf16[1,4,128,1024]{3,1,0,2:T(4,128)(2,1)}), bf16[1,4,128,1024]{3,1,0,2:T(4,128)(2,1)S(1)}, u32[]{:S(2)}, u32[]{:S(2)}) async-start(bf16[1,4,128,1024]{3,1,0,2:T(4,128)(2,1)} %copy.27), calls=%async_computation.1 | async-start | bytes 2097152 | tf_op jit(solution)/shard_map/all_to_all | solution.py:37
  15.1 5.8 %copy-start.9 = (bf16[3,3,256,256]{3,2,1,0:T(8,128)(2,1)S(1)}, bf16[3,3,256,256]{3,2,1,0:T(8,128)(2,1)}, u32[]{:S(2)}) copy-start(bf16[3,3,256,256]{3,2,1,0:T(8,128)(2,1)} %param.9) | copy-start | bytes 3538948
  15.5 6.7 %collective-permute-start.1 = (bf16[1,1,128,256]{3,2,1,0:T(8,128)(2,1)S(1)}, bf16[1,1,128,256]{3,2,1,0:T(8,128)(2,1)S(1)}, u32[]{:S(2)}, u32[]{:S(2)}) collective-permute-start(bf16[1,1,128,256]{3,2,1,0:T(8,128)(2,1)S(1)} %get-tuple-element.50), channel_id=1, source_target_pairs={{1,0},{2,1},{3,2},{5,4},{6,5},{7,6},{9,8},{10,9},{11,10},{13,12},{... | collective-permute-start | bytes 196616 | tf_op jit(solution)/shard_map/ppermute | solution.py:15
  17.6 5.3 %collective-permute-start = (bf16[1,1,128,256]{3,2,1,0:T(8,128)(2,1)S(1)}, bf16[1,1,128,256]{3,2,1,0:T(8,128)(2,1)S(1)}, u32[]{:S(2)}, u32[]{:S(2)}) collective-permute-start(bf16[1,1,128,256]{3,2,1,0:T(8,128)(2,1)S(1)} %get-tuple-element.49), channel_id=1, source_target_pairs={{0,1},{1,2},{2,3},{4,5},{5,6},{6,7},{8,9},{9,10},{10,11},{12,13},{... | collective-permute-start | bytes 196616 | tf_op jit(solution)/shard_map/ppermute | solution.py:14
  23.5 1.4 copy-start.8
  25.4 1.1 copy-start.1
  28.9 8.2 %copy-start.5 = (bf16[1,4,128,1024]{3,1,0,2:T(4,128)(2,1)}, bf16[1,4,128,1024]{3,1,0,2:T(4,128)(2,1)S(1)}, u32[]{:S(2)}) copy-start(bf16[1,4,128,1024]{3,1,0,2:T(4,128)(2,1)S(1)} %all-to-all-done.1) | copy-start | bytes 3145732
  28.9 18.9 %all-to-all-start = ((bf16[1,4,128,1024]{3,1,0,2:T(4,128)(2,1)}), bf16[1,4,128,1024]{3,1,0,2:T(4,128)(2,1)S(1)}, u32[]{:S(2)}, u32[]{:S(2)}) async-start(bf16[1,4,128,1024]{3,1,0,2:T(4,128)(2,1)} %copy.25), calls=%async_computation | async-start | bytes 2097152 | tf_op jit(solution)/shard_map/all_to_all | solution.py:36
  47.8 1.3 copy-start.3
  100.1 3.5 %copy-start.4 = (bf16[1,4,128,1024]{3,1,0,2:T(4,128)(2,1)S(1)}, bf16[1,4,128,1024]{3,1,0,2:T(4,128)(2,1)}, u32[]{:S(2)}) copy-start(bf16[1,4,128,1024]{3,1,0,2:T(4,128)(2,1)} %copy-done.3) | copy-start | bytes 3145732
  109.7 19.2 %all-to-all-start.2 = ((bf16[8,4,16,1024]{3,2,1,0:T(8,128)(2,1)}), bf16[8,4,16,1024]{3,2,1,0:T(8,128)(2,1)S(1)}, u32[]{:S(2)}, u32[]{:S(2)}) async-start(bf16[8,4,16,1024]{3,2,1,0:T(8,128)(2,1)} %fusion.9), calls=%async_computation.2 | async-start | bytes 2097152 | tf_op jit(solution)/shard_map/all_to_all | solution.py:61
  115.0 13.9 %copy-start.2 = (bf16[512,1024]{1,0:T(8,128)(2,1)S(1)}, bf16[512,1024]{1,0:T(8,128)(2,1)}, u32[]{:S(2)}) copy-start(bf16[512,1024]{1,0:T(8,128)(2,1)} %copy-done.1) | copy-start | bytes 3145732
  115.0 38.7 %reduce-scatter.5.cloned.1.call-start = ((), (), s32[]{:S(2)}) async-start(), calls=%async_computation.6 | async-start | bytes 655360 | tf_op jit(solution)/shard_map/reduce_scatter | solution.py:133
  129.7 6.7 %collective-permute-start.3 = (bf16[1,1,128,256]{3,2,1,0:T(8,128)(2,1)S(1)}, bf16[1,1,128,256]{3,2,1,0:T(8,128)(2,1)S(1)}, u32[]{:S(2)}, u32[]{:S(2)}) collective-permute-start(bf16[1,1,128,256]{3,2,1,0:T(8,128)(2,1)S(1)} %get-tuple-element.46), channel_id=1, source_target_pairs={{1,0},{2,1},{3,2},{5,4},{6,5},{7,6},{9,8},{10,9},{11,10},{13,12},{... | collective-permute-start | bytes 196616 | tf_op jit(solution)/shard_map/ppermute | solution.py:15
  131.8 5.0 %collective-permute-start.2 = (bf16[1,1,128,256]{3,2,1,0:T(8,128)(2,1)S(1)}, bf16[1,1,128,256]{3,2,1,0:T(8,128)(2,1)S(1)}, u32[]{:S(2)}, u32[]{:S(2)}) collective-permute-start(bf16[1,1,128,256]{3,2,1,0:T(8,128)(2,1)S(1)} %get-tuple-element.45), channel_id=1, source_target_pairs={{0,1},{1,2},{2,3},{4,5},{5,6},{6,7},{8,9},{9,10},{10,11},{12,13},{... | collective-permute-start | bytes 196616 | tf_op jit(solution)/shard_map/ppermute | solution.py:14
  136.3 40.1 %reduce-scatter.3.cloned.1.call-start = ((), (), s32[]{:S(2)}) async-start(), calls=%async_computation.5 | async-start | bytes 655360 | tf_op jit(solution)/shard_map/reduce_scatter | solution.py:130
  137.4 2.2 copy-start.7
  140.9 108.2 %all-reduce.8.cloned.1.call-start = ((), (), s32[]{:S(2)}) async-start(), calls=%async_computation.7 | async-start | bytes 3145728
  147.7 2.3 copy-start.12
Sparse Core Ops, SparseCore 0:
  136.4 17.0 reduce-scatter.4
  156.4 19.9 reduce-scatter.2
  178.8 70.3 all-reduce.7
where the time goes:
time: 261 us; the launch traced here: 258 us
  waiting for transfers between devices  103 us (39%)
  local copies, waits for them, and re-layouts  43.9 us (17%)
  blocking collectives  39.4 us (15%)
  starting transfers between devices  25.8 us (10%)
  other arithmetic  18.6 us (7%)
  between operations  14.8 us (6%)
  matrix products  11.8 us (5%)
    unnamed x4, waiting for transfers between devices  71.1 us
    psum x1, blocking collectives, slices_route(): lax.psum((gram_table(student_rows, partners), gram_table(teacher_rows, pa...  39.4 us
    reduce_scatter x1, waiting for transfers between devices, body(): lax.psum_scatter(local_reduce[None].astype(jnp.bfloat16), 'space', scatte...  21.1 us
    unnamed x54, local copies, waits for them, and re-layouts  19.4 us
    gather x4, local copies, waits for them, and re-layouts, gram_table(): features[partners[round_index]]  7.9 us
    all_to_all x1, waiting for transfers between devices, slices_route(): lax.all_to_all(grad_cut, 'dp', split_axis=0, concat_axis=2, tiled=True)  7.37 us
    ppermute x2, starting transfers between devices, extended(): before = lax.ppermute(last, axis, up)  6.34 us
    convert_element_type x1, other arithmetic, slices_route(): (elems_total * summed).astype(jnp.bfloat16).reshape(student_cut.shape)  6 us
  transfers between devices with their start and end apart: 10, of which 7 were waited for; matrix products, arithmetic and copies ran while one was open for 17% of the time, Pallas kernels for 0%

commit v1 on v0

v1 whole, which is shorter than its diff:
```python
import functools

import jax
import jax.numpy as jnp
from jax import lax
from jax.experimental import pallas as pl
from jax.experimental.pallas import tpu as pltpu
from jax.sharding import PartitionSpec as P

MESH = pl.DeviceIdType.MESH
F32 = jnp.float32
BF16 = jnp.bfloat16


def mm(a, b, ca=1, cb=0):
    return lax.dot_general(a, b, (((ca,), (cb,)), ((), ())), preferred_element_type=F32)


def kernel(
    dims, part, x, t, wr, ws, we,
    loss_o, gi_o, gr_o, gs_o, ge_o,
    h1, h2, st, patch, g2, xt, h2t, up, down, up2, down2,
    tcut, scut, gcut, gpre, gram, slots, zsend, zslots, coef,
    grp, gsp, gep, grr, gsr, ger,
    t_send, t_recv, s_send, s_recv, g_send, g_recv, v_send, v_recv,
    z_send, z_recv, e_send, e_recv, r_send, r_recv,
):
    dp, sp, rows, cols, elems = dims
    chans, mid = wr.shape
    pixels = rows * cols
    span = pixels // dp
    me = lax.axis_index("dp")
    my = lax.axis_index("space")

    def dp_peer(shift):
        return lax.rem(me + shift, dp)

    def sp_peer(shift):
        return lax.rem(my + shift, sp)

    def remote(src, dst, send, recv, where):
        return pltpu.make_async_remote_copy(
            src_ref=src, dst_ref=dst, send_sem=send, recv_sem=recv,
            device_id=where, device_id_type=MESH,
        )

    up[...] = jnp.zeros_like(up)
    down[...] = jnp.zeros_like(down)
    up2[...] = jnp.zeros_like(up2)
    down2[...] = jnp.zeros_like(down2)

    barrier = pltpu.get_barrier_semaphore()
    for shift in range(1, dp):
        pl.semaphore_signal(
            barrier, inc=1, device_id={"dp": dp_peer(shift)}, device_id_type=MESH
        )
    for shift in range(1, sp):
        pl.semaphore_signal(
            barrier, inc=1, device_id={"space": sp_peer(shift)}, device_id_type=MESH
        )
    pl.semaphore_wait(barrier, dp + sp - 2)

    def cut_copy(src, dst, send, recv, shift):
        peer = dp_peer(shift)
        return remote(
            src.at[pl.ds(pl.multiple_of(peer * span, span), span)],
            dst.at[me], send.at[shift - 1], recv.at[shift - 1], {"dp": peer},
        )

    def cut_arrival(src, dst, send, recv, shift):
        origin = lax.rem(me + dp - shift, dp)
        return remote(
            src.at[pl.ds(0, span)], dst.at[origin],
            send.at[shift - 1], recv.at[shift - 1], {"dp": origin},
        )

    mine = pl.ds(pl.multiple_of(me * span, span), span)
    for shift in range(1, dp):
        cut_copy(t, tcut, t_send, t_recv, shift).start()
    tcut[me] = t[mine, :]

    def edges(src, above, below, base, act):
        first, last = src.at[pl.ds(0, cols)], src.at[pl.ds(pixels - cols, cols)]

        def move(part_rows, dst, slot, peer):
            return remote(
                part_rows, dst, e_send.at[slot], e_recv.at[slot], {"space": peer}
            )

        @pl.when(my > 0)
        def _():
            if act == "start":
                move(first, below, base, my - 1).start()
            elif act == "recv":
                move(first, above, base + 1, my - 1).wait_recv()
            else:
                move(first, below, base, my - 1).wait_send()

        @pl.when(my < sp - 1)
        def _():
            if act == "start":
                move(last, above, base + 1, my + 1).start()
            elif act == "recv":
                move(last, below, base, my + 1).wait_recv()
            else:
                move(last, above, base + 1, my + 1).wait_send()

    column = lax.broadcasted_iota(jnp.int32, (cols, mid), 0)

    def place(value, row):
        wide = value.astype(F32)
        left = jnp.where(column == 0, 0.0, pltpu.roll(wide, 1, 0)).astype(BF16)
        right = jnp.where(column == cols - 1, 0.0, pltpu.roll(wide, cols - 1, 0)).astype(BF16)
        for a in range(3):
            to = row - a + 1
            if 0 <= to < rows:
                for b, piece in enumerate((left, value, right)):
                    tap = a * 3 + b
                    patch[to * cols:(to + 1) * cols, tap * mid:(tap + 1) * mid] = piece

    h1[...] = jnp.maximum(mm(x[...], wr[...]), 0.0).astype(BF16)
    edges(h1, up, down, 0, "start")
    for row in range(rows):
        place(h1[row * cols:(row + 1) * cols, :], row)
    edges(h1, up, down, 0, "recv")
    place(up[...], -1)
    place(down[...], rows)
    h2[...] = jnp.maximum(mm(patch[...], ws[...]), 0.0).astype(BF16)
    for row in range(rows):
        at = slice(row * cols, (row + 1) * cols)
        st[at, :] = jnp.maximum(mm(h2[at, :], we[...]) + x[at, :].astype(F32), 0.0).astype(BF16)
    for shift in range(1, dp):
        cut_copy(st, scut, s_send, s_recv, shift).start()
    scut[me] = st[mine, :]

    lane = lax.broadcasted_iota(jnp.int32, (1, 128), 1)

    def gram_rows(cut, first):
        def one(i, carry):
            others = [part[0, i], part[1, i]]
            sums = [jnp.zeros((8, 128), F32) for _ in range(3)]
            for block in range(chans // 128):
                at = slice(block * 128, (block + 1) * 128)
                own = cut[i, :, at].astype(F32)
                for j, right in enumerate(
                    (own, cut[others[0], :, at].astype(F32), cut[others[1], :, at].astype(F32))
                ):
                    sums[j] = sums[j] + jnp.sum((own * right).reshape(span // 8, 8, 128), axis=0)
            line = jnp.zeros((1, 128), F32)
            for j in range(3):
                total = jnp.sum(jnp.sum(sums[j], axis=0, keepdims=True), axis=1, keepdims=True)
                line = jnp.where(lane == first + j, total, line)
            if first:
                gram[pl.ds(i, 1), :] = jnp.where(lane >= first, line, gram[pl.ds(i, 1), :])
            else:
                gram[pl.ds(i, 1), :] = line
            return carry

        lax.fori_loop(0, dp, one, 0)

    for shift in range(1, dp):
        cut_arrival(t, tcut, t_send, t_recv, shift).wait_recv()
    gram_rows(tcut, 0)
    xt[...] = x[...].T
    h2t[...] = h2[...].T
    for shift in range(1, dp):
        cut_arrival(st, scut, s_send, s_recv, shift).wait_recv()
    gram_rows(scut, 3)

    def gram_copy(shift):
        return remote(
            gram, slots.at[me], v_send.at[shift - 1], v_recv.at[shift - 1],
            {"dp": dp_peer(shift)},
        )

    for shift in range(1, dp):
        gram_copy(shift).start()
    slots[me] = gram[...]
    for shift in range(1, dp):
        origin = lax.rem(me + dp - shift, dp)
        remote(
            gram, slots.at[origin], v_send.at[shift - 1], v_recv.at[shift - 1], {"dp": origin}
        ).wait_recv()
    total = slots[0]
    for k in range(1, dp):
        total = total + slots[k]
    zsend[...] = total

    def sum_copy(shift):
        return remote(
            zsend, zslots.at[my], z_send.at[shift - 1], z_recv.at[shift - 1],
            {"space": sp_peer(shift)},
        )

    for shift in range(1, sp):
        sum_copy(shift).start()
    zslots[my] = total
    for shift in range(1, sp):
        origin = lax.rem(my + sp - shift, sp)
        remote(
            zsend, zslots.at[origin], z_send.at[shift - 1], z_recv.at[shift - 1],
            {"space": origin},
        ).wait_recv()
    total = zslots[0]
    for k in range(1, sp):
        total = total + zslots[k]
    lanes = lax.broadcasted_iota(jnp.int32, (dp, 128), 1)

    def spread(j):
        one = jnp.sum(jnp.where(lanes == j, total, 0.0), axis=1, keepdims=True)
        return jnp.broadcast_to(one, (dp, 128))

    v_t = [spread(j) for j in range(3)]
    v_s = [spread(3 + j) for j in range(3)]
    nu_t = jnp.sqrt(v_t[0] * v_t[0] + v_t[1] * v_t[1] + v_t[2] * v_t[2] + 1e-06)
    nu_s = jnp.sqrt(v_s[0] * v_s[0] + v_s[1] * v_s[1] + v_s[2] * v_s[2] + 1e-06)
    n_s = [v / nu_s for v in v_s]
    diff = [a - b / nu_t for a, b in zip(n_s, v_t)]
    loss = diff[0] * diff[0] + diff[1] * diff[1] + diff[2] * diff[2]
    loss_o[...] = jnp.sum(loss, axis=0, keepdims=True)
    err = [2.0 * d for d in diff]
    along = err[0] * n_s[0] + err[1] * n_s[1] + err[2] * n_s[2]
    for j in range(3):
        coef[j] = (err[j] - along * n_s[j]) / nu_s

    def grad_slice(i):
        one, two = part[0, i], part[1, i]
        weights = (
            2.0 * coef[0, pl.ds(i, 1), :],
            coef[1, pl.ds(i, 1), :] + coef[1, pl.ds(one, 1), :],
            coef[2, pl.ds(i, 1), :] + coef[2, pl.ds(two, 1), :],
        )
        for block in range(chans // 128):
            at = slice(block * 128, (block + 1) * 128)
            own = scut[i, :, at].astype(F32)
            summed = weights[0] * own
            summed = summed + weights[1] * scut[one, :, at].astype(F32)
            summed = summed + weights[2] * scut[two, :, at].astype(F32)
            gcut[i, :, at] = jnp.where(own > 0, elems * summed, 0.0).astype(BF16)

    def grad_copy(shift):
        peer = dp_peer(shift)
        return remote(
            gcut.at[peer], gpre.at[mine], g_send.at[shift - 1], g_recv.at[shift - 1],
            {"dp": peer},
        )

    def send_slice(shift, carry):
        grad_slice(dp_peer(shift))
        grad_copy(shift).start()
        return carry

    lax.fori_loop(1, dp, send_slice, 0)
    grad_slice(me)
    gpre[mine, :] = gcut[me]
    for shift in range(1, dp):
        origin = lax.rem(me + dp - shift, dp)
        remote(
            gcut.at[origin], gpre.at[pl.ds(pl.multiple_of(origin * span, span), span)],
            g_send.at[shift - 1], g_recv.at[shift - 1], {"dp": origin},
        ).wait_recv()

    g2[...] = jnp.where(h2[...] > 0, mm(gpre[...], we[...], 1, 1), 0.0).astype(BF16)
    edges(g2, up2, down2, 2, "start")

    width = chans // sp
    depth = mid // sp

    def ge_copy(shift):
        return remote(
            gep.at[sp_peer(shift)], ger.at[shift - 1], r_send.at[0, shift - 1],
            r_recv.at[0, shift - 1], {"space": sp_peer(shift)},
        )

    def gs_copy(shift):
        peer = sp_peer(shift)
        return remote(
            gsp.at[pl.ds(pl.multiple_of(peer * depth, depth), depth)], gsr.at[shift - 1],
            r_send.at[1, shift - 1], r_recv.at[1, shift - 1], {"space": peer},
        )

    def gr_copy(shift):
        peer = sp_peer(shift)
        return remote(
            grp.at[pl.ds(pl.multiple_of(peer * width, width), width)], grr.at[shift - 1],
            r_send.at[2, shift - 1], r_recv.at[2, shift - 1], {"space": peer},
        )

    for k in range(sp):
        gep[k] = mm(h2t[...], gpre[:, k * width:(k + 1) * width]).astype(BF16)
    for shift in range(1, sp):
        ge_copy(shift).start()
    g2t = g2[...].T
    for tap in range(9):
        at = slice(tap * mid, (tap + 1) * mid)
        gsp[:, at] = mm(g2t, patch[:, at]).astype(BF16)
    for shift in range(1, sp):
        gs_copy(shift).start()

    for row in range(rows):
        place(g2[row * cols:(row + 1) * cols, :], row)
    edges(g2, up2, down2, 2, "recv")
    place(up2[...], -1)
    place(down2[...], rows)
    back = None
    for tap in range(9):
        flip = 8 - tap
        term = mm(
            patch[:, tap * mid:(tap + 1) * mid], ws[flip * mid:(flip + 1) * mid, :], 1, 1
        )
        back = term if back is None else back + term
    edges(h1, up, down, 0, "send")
    g1 = jnp.where(h1[...] > 0, back, 0.0).astype(BF16)
    grp[...] = mm(xt[...], g1).astype(BF16)
    for shift in range(1, sp):
        gr_copy(shift).start()
    h1[...] = g1
    for row in range(rows):
        at = slice(row * cols, (row + 1) * cols)
        gi_o[at, :] = (gpre[at, :].astype(F32) + mm(h1[at, :], wr[...], 1, 1)).astype(BF16)

    for shift in range(1, sp):
        ge_copy(shift).wait_recv()
    ge = gep[my].astype(F32)
    for k in range(sp - 1):
        ge = ge + ger[k].astype(F32)
    ge_o[...] = ge
    for shift in range(1, sp):
        gs_copy(shift).wait_recv()
    at_rows = pl.ds(pl.multiple_of(my * depth, depth), depth)
    for tap in range(9):
        at = slice(tap * mid, (tap + 1) * mid)
        gs = gsp[at_rows, at].astype(F32)
        for k in range(sp - 1):
            gs = gs + gsr[k, :, at].astype(F32)
        gs_o[tap] = gs
    for shift in range(1, sp):
        gr_copy(shift).wait_recv()
    gr = grp[pl.ds(pl.multiple_of(my * width, width), width), :].astype(F32)
    for k in range(sp - 1):
        gr = gr + grr[k].astype(F32)
    gr_o[...] = gr

    for shift in range(1, dp):
        cut_copy(t, tcut, t_send, t_recv, shift).wait_send()
        cut_copy(st, scut, s_send, s_recv, shift).wait_send()
        gram_copy(shift).wait_send()
        grad_copy(shift).wait_send()
    edges(g2, up2, down2, 2, "send")
    for shift in range(1, sp):
        sum_copy(shift).wait_send()
        ge_copy(shift).wait_send()
        gs_copy(shift).wait_send()
        gr_copy(shift).wait_send()


def body(images, teacher, w_reduce, w_spatial, w_expand, partners):
    dp, sp = lax.axis_size("dp"), lax.axis_size("space")
    _, rows, cols, chans = images.shape
    mid = w_reduce.shape[1]
    pixels = rows * cols
    span, width, depth = pixels // dp, chans // sp, mid // sp
    elems = float(rows * sp * cols * chans)
    vmem = pl.BlockSpec(memory_space=pltpu.VMEM)
    dma = pltpu.SemaphoreType.DMA
    loss, gi, gr, gs, ge = pl.pallas_call(
        functools.partial(kernel, (dp, sp, rows, cols, elems)),
        out_shape=(
            jax.ShapeDtypeStruct((1, 128), F32),
            jax.ShapeDtypeStruct((pixels, chans), BF16),
            jax.ShapeDtypeStruct((width, mid), F32),
            jax.ShapeDtypeStruct((9, depth, mid), F32),
            jax.ShapeDtypeStruct((mid, width), F32),
        ),
        in_specs=[pl.BlockSpec(memory_space=pltpu.SMEM)] + [vmem] * 5,
        out_specs=(vmem,) * 5,
        scratch_shapes=[
            pltpu.VMEM((pixels, mid), BF16),
            pltpu.VMEM((pixels, mid), BF16),
            pltpu.VMEM((pixels, chans), BF16),
            pltpu.VMEM((pixels, 9 * mid), BF16),
            pltpu.VMEM((pixels, mid), BF16),
            pltpu.VMEM((chans, pixels), BF16),
            pltpu.VMEM((mid, pixels), BF16),
            pltpu.VMEM((cols, mid), BF16),
            pltpu.VMEM((cols, mid), BF16),
            pltpu.VMEM((cols, mid), BF16),
            pltpu.VMEM((cols, mid), BF16),
            pltpu.VMEM((dp, span, chans), BF16),
            pltpu.VMEM((dp, span, chans), BF16),
            pltpu.VMEM((dp, span, chans), BF16),
            pltpu.VMEM((pixels, chans), BF16),
            pltpu.VMEM((dp, 128), F32),
            pltpu.VMEM((dp, dp, 128), F32),
            pltpu.VMEM((dp, 128), F32),
            pltpu.VMEM((sp, dp, 128), F32),
            pltpu.VMEM((3, dp, 128), F32),
            pltpu.VMEM((chans, mid), BF16),
            pltpu.VMEM((mid, 9 * mid), BF16),
            pltpu.VMEM((sp, mid, width), BF16),
            pltpu.VMEM((sp - 1, width, mid), BF16),
            pltpu.VMEM((sp - 1, depth, 9 * mid), BF16),
            pltpu.VMEM((sp - 1, mid, width), BF16),
            dma((dp - 1,)), dma((dp - 1,)), dma((dp - 1,)), dma((dp - 1,)),
            dma((dp - 1,)), dma((dp - 1,)), dma((dp - 1,)), dma((dp - 1,)),
            dma((sp - 1,)), dma((sp - 1,)), dma((4,)), dma((4,)),
            dma((3, sp - 1)), dma((3, sp - 1)),
        ],
        compiler_params=pltpu.CompilerParams(
            collective_id=0, has_side_effects=True, vmem_limit_bytes=48 * 1024 * 1024
        ),
        name="distill",
    )(
        partners,
        images.reshape(pixels, chans),
        teacher.reshape(pixels, chans),
        w_reduce,
        w_spatial.reshape(9 * mid, mid),
        w_expand,
    )
    return (
        loss[0, 0],
        gi.reshape(images.shape),
        gr[None],
        gs.reshape(1, 3, 3, depth, mid).transpose(0, 1, 2, 4, 3),
        ge[None],
    )


def solution(mesh):
    return jax.shard_map(
        body,
        mesh=mesh,
        in_specs=(P("dp", "space", None, None), P("dp", "space", None, None), P(), P(), P(), P()),
        out_specs=(
            P(),
            P("dp", "space", None, None),
            P("dp", "space", None),
            P("dp", None, None, None, "space"),
            P("dp", None, "space"),
        ),
        check_vma=False,
    )
```

time: 261 us -> 111 us (0.43); the launches traced: 258 us -> 111 us
  waiting for transfers between devices: 103 us -> 0 us
  Pallas kernels: 0 us -> 100 us
  blocking collectives: 39.4 us -> 0 us
  local copies, waits for them, and re-layouts: 43.9 us -> 8.39 us
  starting transfers between devices: 25.8 us -> 0 us
  other arithmetic: 18.6 us -> 0 us
  between operations: 14.8 us -> 1.82 us
  matrix products: 11.8 us -> 0 us
    pallas_call x0 -> x1, Pallas kernels: none -> 100 us  [body(): pl.pallas_call(functools.partial(kernel, (dp, sp, rows, cols, elems)), ou...]
    unnamed x4 -> x0, waiting for transfers between devices: 71.1 us -> none
    psum x1 -> x0, blocking collectives: 39.4 us -> none  [slices_route(): lax.psum((gram_table(student_rows, partners), gram_table(teacher_rows, pa...]
    reduce_scatter x2 -> x0, waiting for transfers between devices: 21.1 us -> none  [the longest x1 21.1 us: body(): lax.psum_scatter(local_reduce[None].astype(jnp.bfloat16), 'space', scatte...]
    all_to_all x3 -> x0, starting transfers between devices: 15.1 us -> none  [the longest x1 5.36 us: slices_route(): lax.all_to_all(grad_cut, 'dp', split_axis=0, concat_axis=2, tiled=True)]
    convert_element_type x5 -> x0, other arithmetic: 13.1 us -> none  [the longest x1 6 us: slices_route(): (elems_total * summed).astype(jnp.bfloat16).reshape(student_cut.shape)]
    dot_general x9 -> x0, matrix products: 11.8 us -> none  [the longest x1 2.49 us: body(): jnp.dot(g_one, w_reduce.T, preferred_element_type=jnp.float32)]
    unnamed x54 -> x14, local copies, waits for them, and re-layouts: 19.4 us -> 8.39 us
  transfers between devices with their start and end apart: 10 -> 0, of which waited for: 7 -> 0; matrix products, arithmetic and copies ran while one was open for 17% -> 0% of each run, Pallas kernels for 0% -> 0%
where the time goes in v1:
time: 111 us
  Pallas kernels  100 us (90%)
  local copies, waits for them, and re-layouts  8.39 us (8%)
  between operations  1.82 us (2%)
    pallas_call x1, Pallas kernels, body(): pl.pallas_call(functools.partial(kernel, (dp, sp, rows, cols, elems)), ou...  100 us
    unnamed x14, local copies, waits for them, and re-layouts  8.39 us

profile of v1, /device:TPU:11, one launch (start us, length us, event | category | flops | bytes accessed | tf_op | source)
XLA Modules:
  0.0 110.6 jit_solution(17335798879612742143)
XLA Ops:
  0.6 0.0 copy-start
  0.6 1.2 %copy-done = bf16[1,4,128,1024]{3,2,1,0:T(8,128)(2,1)S(1)} copy-done((bf16[1,4,128,1024]{3,2,1,0:T(8,128)(2,1)S(1)}, bf16[1,4,128,1024]{3,2,1,0:T(8,128)(2,1)}, u32[]{:S(2)}) %copy-start) | copy-done | bytes 1048600
  1.9 0.0 copy-start.1
  1.9 1.2 %copy-done.1 = bf16[1,4,128,1024]{3,2,1,0:T(8,128)(2,1)S(1)} copy-done((bf16[1,4,128,1024]{3,2,1,0:T(8,128)(2,1)S(1)}, bf16[1,4,128,1024]{3,2,1,0:T(8,128)(2,1)}, u32[]{:S(2)}) %copy-start.1) | copy-done | bytes 1048600
  3.1 0.0 copy-start.2
  3.1 1.0 copy-done.2
  4.1 0.0 copy-start.3
  4.1 1.0 copy-done.3
  5.2 0.0 copy-start.4
  5.2 0.7 copy-done.4
  5.8 100.4 %distill.1 = (f32[1,128]{1,0:T(1,128)S(1)}, bf16[512,1024]{1,0:T(8,128)(2,1)S(1)}, f32[256,256]{1,0:T(8,128)S(1)}, f32[9,64,256]{2,1,0:T(8,128)S(1)}, f32[256,256]{1,0:T(8,128)S(1)}) custom-call(s32[2,8]{1,0:T(2,128)S(1)} %copy-done.4, bf16[512,1024]{1,0:T(8,128)(2,1)S(1)} %bitcast.11, bf16[512,1024]{1,0:T(8,128)(2,1)S(1)} %bitcast.12, ...), custom_call_target="tpu_custom_call" | custom-call | tf_op jit(solution)/shard_map/distill/pallas_call | solution.py:366
  106.3 1.0 copy.17
  107.3 0.7 copy.18
  108.0 0.8 copy.19
  108.8 0.7 copy.20
Async XLA Ops:
  0.6 1.2 %copy-start = (bf16[1,4,128,1024]{3,2,1,0:T(8,128)(2,1)S(1)}, bf16[1,4,128,1024]{3,2,1,0:T(8,128)(2,1)}, u32[]{:S(2)}) copy-start(bf16[1,4,128,1024]{3,2,1,0:T(8,128)(2,1)} %param.6) | copy-start | bytes 3145732
  1.9 1.2 %copy-start.1 = (bf16[1,4,128,1024]{3,2,1,0:T(8,128)(2,1)S(1)}, bf16[1,4,128,1024]{3,2,1,0:T(8,128)(2,1)}, u32[]{:S(2)}) copy-start(bf16[1,4,128,1024]{3,2,1,0:T(8,128)(2,1)} %param.7) | copy-start | bytes 3145732
  3.1 1.0 copy-start.2
  4.1 1.0 copy-start.3
  5.2 0.7 copy-start.4

commit v2 on v1

--- a/solution.py
+++ b/solution.py
@@ -17,16 +17,16 @@
 
 
 def kernel(
-    dims, part, x, t, wr, ws, we,
+    dims, part, x_hbm, t, wr_hbm, ws_hbm, we_hbm,
     loss_o, gi_o, gr_o, gs_o, ge_o,
-    h1, h2, st, patch, g2, xt, h2t, up, down, up2, down2,
+    x, wr, ws, we, h1, g1, h1f, g2t, g2f, h2, st, patch, g2, xt, h2t, up, down, up2, down2,
     tcut, scut, gcut, gpre, gram, slots, zsend, zslots, coef,
-    grp, gsp, gep, grr, gsr, ger,
+    grp, gep, grr, ger,
     t_send, t_recv, s_send, s_recv, g_send, g_recv, v_send, v_recv,
-    z_send, z_recv, e_send, e_recv, r_send, r_recv,
+    z_send, z_recv, e_send, e_recv, r_send, r_recv, l_sem,
 ):
     dp, sp, rows, cols, elems = dims
-    chans, mid = wr.shape
+    chans, mid = wr_hbm.shape
     pixels = rows * cols
     span = pixels // dp
     me = lax.axis_index("dp")
@@ -44,6 +44,12 @@
             device_id=where, device_id_type=MESH,
         )
 
+    loads = [
+        pltpu.make_async_copy(src, dst, l_sem.at[k])
+        for k, (src, dst) in enumerate(((x_hbm, x), (wr_hbm, wr), (ws_hbm, ws), (we_hbm, we)))
+    ]
+    for load in loads:
+        load.start()
     up[...] = jnp.zeros_like(up)
     down[...] = jnp.zeros_like(down)
     up2[...] = jnp.zeros_like(up2)
@@ -77,7 +83,8 @@
     mine = pl.ds(pl.multiple_of(me * span, span), span)
     for shift in range(1, dp):
         cut_copy(t, tcut, t_send, t_recv, shift).start()
-    tcut[me] = t[mine, :]
+    own_cut = pltpu.make_async_copy(t.at[mine], tcut.at[me], l_sem.at[4])
+    own_cut.start()
 
     def edges(src, above, below, base, act):
         first, last = src.at[pl.ds(0, cols)], src.at[pl.ds(pixels - cols, cols)]
@@ -118,13 +125,49 @@
                     tap = a * 3 + b
                     patch[to * cols:(to + 1) * cols, tap * mid:(tap + 1) * mid] = piece
 
+    depth = mid // sp
+
+    def h1_copy(shift):
+        return remote(
+            h1, h1f.at[pl.ds(pl.multiple_of(my * pixels, pixels), pixels)],
+            r_send.at[1, shift - 1], r_recv.at[1, shift - 1], {"space": sp_peer(shift)},
+        )
+
+    def h1_arrival(shift):
+        origin = lax.rem(my + sp - shift, sp)
+        return remote(
+            h1, h1f.at[pl.ds(pl.multiple_of(origin * pixels, pixels), pixels)],
+            r_send.at[1, shift - 1], r_recv.at[1, shift - 1], {"space": origin},
+        )
+
+    def g2_copy(shift):
+        peer = sp_peer(shift)
+        return remote(
+            g2t.at[pl.ds(pl.multiple_of(peer * depth, depth), depth)], g2f.at[my],
+            r_send.at[3, shift - 1], r_recv.at[3, shift - 1], {"space": peer},
+        )
+
+    def g2_arrival(shift):
+        origin = lax.rem(my + sp - shift, sp)
+        return remote(
+            g2t.at[pl.ds(0, depth)], g2f.at[origin],
+            r_send.at[3, shift - 1], r_recv.at[3, shift - 1], {"space": origin},
+        )
+
+    loads[0].wait()
+    loads[1].wait()
     h1[...] = jnp.maximum(mm(x[...], wr[...]), 0.0).astype(BF16)
     edges(h1, up, down, 0, "start")
+    for shift in range(1, sp):
+        h1_copy(shift).start()
+    h1f[pl.ds(pl.multiple_of(my * pixels, pixels), pixels), :] = h1[...]
     for row in range(rows):
         place(h1[row * cols:(row + 1) * cols, :], row)
     edges(h1, up, down, 0, "recv")
     place(up[...], -1)
     place(down[...], rows)
+    loads[2].wait()
+    loads[3].wait()
     h2[...] = jnp.maximum(mm(patch[...], ws[...]), 0.0).astype(BF16)
     for row in range(rows):
         at = slice(row * cols, (row + 1) * cols)
@@ -160,6 +203,7 @@
 
     for shift in range(1, dp):
         cut_arrival(t, tcut, t_send, t_recv, shift).wait_recv()
+    own_cut.wait()
     gram_rows(tcut, 0)
     xt[...] = x[...].T
     h2t[...] = h2[...].T
@@ -264,7 +308,9 @@
     edges(g2, up2, down2, 2, "start")
 
     width = chans // sp
-    depth = mid // sp
+    g2t[...] = g2[...].T
+    for shift in range(1, sp):
+        g2_copy(shift).start()
 
     def ge_copy(shift):
         return remote(
@@ -272,13 +318,6 @@
             r_recv.at[0, shift - 1], {"space": sp_peer(shift)},
         )
 
-    def gs_copy(shift):
-        peer = sp_peer(shift)
-        return remote(
-            gsp.at[pl.ds(pl.multiple_of(peer * depth, depth), depth)], gsr.at[shift - 1],
-            r_send.at[1, shift - 1], r_recv.at[1, shift - 1], {"space": peer},
-        )
-
     def gr_copy(shift):
         peer = sp_peer(shift)
         return remote(
@@ -290,12 +329,7 @@
         gep[k] = mm(h2t[...], gpre[:, k * width:(k + 1) * width]).astype(BF16)
     for shift in range(1, sp):
         ge_copy(shift).start()
-    g2t = g2[...].T
-    for tap in range(9):
-        at = slice(tap * mid, (tap + 1) * mid)
-        gsp[:, at] = mm(g2t, patch[:, at]).astype(BF16)
-    for shift in range(1, sp):
-        gs_copy(shift).start()
+    g2f[my] = g2t[pl.ds(pl.multiple_of(my * depth, depth), depth), :]
 
     for row in range(rows):
         place(g2[row * cols:(row + 1) * cols, :], row)
@@ -309,15 +343,41 @@
             patch[:, tap * mid:(tap + 1) * mid], ws[flip * mid:(flip + 1) * mid, :], 1, 1
         )
         back = term if back is None else back + term
-    edges(h1, up, down, 0, "send")
-    g1 = jnp.where(h1[...] > 0, back, 0.0).astype(BF16)
-    grp[...] = mm(xt[...], g1).astype(BF16)
+    g1[...] = jnp.where(h1[...] > 0, back, 0.0).astype(BF16)
+    grp[...] = mm(xt[...], g1[...]).astype(BF16)
     for shift in range(1, sp):
         gr_copy(shift).start()
-    h1[...] = g1
     for row in range(rows):
         at = slice(row * cols, (row + 1) * cols)
-        gi_o[at, :] = (gpre[at, :].astype(F32) + mm(h1[at, :], wr[...], 1, 1)).astype(BF16)
+        gi_o[at, :] = (gpre[at, :].astype(F32) + mm(g1[at, :], wr[...], 1, 1)).astype(BF16)
+
+    for shift in range(1, sp):
+        h1_arrival(shift).wait_recv()
+        g2_arrival(shift).wait_recv()
+    spot = lax.broadcasted_iota(jnp.int32, (depth, cols), 1)
+    ahead, centre, behind = [], [], []
+    for k in range(sp):
+        for row in range(rows):
+            piece = g2f[k, :, row * cols:(row + 1) * cols]
+            wide = piece.astype(F32)
+            ahead.append(
+                jnp.where(spot == cols - 1, 0.0, pltpu.roll(wide, cols - 1, 1)).astype(BF16)
+            )
+            centre.append(piece)
+            behind.append(jnp.where(spot == 0, 0.0, pltpu.roll(wide, 1, 1)).astype(BF16))
+    stack = jnp.concatenate(
+        [jnp.concatenate(line, axis=1) for line in (ahead, centre, behind)], axis=0
+    )
+    every = sp * pixels
+    for a in range(3):
+        if a == 0:
+            part_sum = mm(stack[:, cols:], h1f[0:every - cols, :])
+        elif a == 1:
+            part_sum = mm(stack, h1f[...])
+        else:
+            part_sum = mm(stack[:, :every - cols], h1f[cols:every, :])
+        for b in range(3):
+            gs_o[a * 3 + b] = part_sum[b * depth:(b + 1) * depth]
 
     for shift in range(1, sp):
         ge_copy(shift).wait_recv()
@@ -326,15 +386,6 @@
         ge = ge + ger[k].astype(F32)
     ge_o[...] = ge
     for shift in range(1, sp):
-        gs_copy(shift).wait_recv()
-    at_rows = pl.ds(pl.multiple_of(my * depth, depth), depth)
-    for tap in range(9):
-        at = slice(tap * mid, (tap + 1) * mid)
-        gs = gsp[at_rows, at].astype(F32)
-        for k in range(sp - 1):
-            gs = gs + gsr[k, :, at].astype(F32)
-        gs_o[tap] = gs
-    for shift in range(1, sp):
         gr_copy(shift).wait_recv()
     gr = grp[pl.ds(pl.multiple_of(my * width, width), width), :].astype(F32)
     for k in range(sp - 1):
@@ -346,11 +397,13 @@
         cut_copy(st, scut, s_send, s_recv, shift).wait_send()
         gram_copy(shift).wait_send()
         grad_copy(shift).wait_send()
+    edges(h1, up, down, 0, "send")
     edges(g2, up2, down2, 2, "send")
     for shift in range(1, sp):
         sum_copy(shift).wait_send()
         ge_copy(shift).wait_send()
-        gs_copy(shift).wait_send()
+        h1_copy(shift).wait_send()
+        g2_copy(shift).wait_send()
         gr_copy(shift).wait_send()
 
 
@@ -372,10 +425,18 @@
             jax.ShapeDtypeStruct((9, depth, mid), F32),
             jax.ShapeDtypeStruct((mid, width), F32),
         ),
-        in_specs=[pl.BlockSpec(memory_space=pltpu.SMEM)] + [vmem] * 5,
+        in_specs=[pl.BlockSpec(memory_space=pltpu.SMEM)] + [pl.BlockSpec(memory_space=pl.ANY)] * 5,
         out_specs=(vmem,) * 5,
         scratch_shapes=[
+            pltpu.VMEM((pixels, chans), BF16),
+            pltpu.VMEM((chans, mid), BF16),
+            pltpu.VMEM((9 * mid, mid), BF16),
+            pltpu.VMEM((mid, chans), BF16),
             pltpu.VMEM((pixels, mid), BF16),
+            pltpu.VMEM((pixels, mid), BF16),
+            pltpu.VMEM((sp * pixels, mid), BF16),
+            pltpu.VMEM((mid, pixels), BF16),
+            pltpu.VMEM((sp, depth, pixels), BF16),
             pltpu.VMEM((pixels, mid), BF16),
             pltpu.VMEM((pixels, chans), BF16),
             pltpu.VMEM((pixels, 9 * mid), BF16),
@@ -396,15 +457,13 @@
             pltpu.VMEM((sp, dp, 128), F32),
             pltpu.VMEM((3, dp, 128), F32),
             pltpu.VMEM((chans, mid), BF16),
-            pltpu.VMEM((mid, 9 * mid), BF16),
             pltpu.VMEM((sp, mid, width), BF16),
             pltpu.VMEM((sp - 1, width, mid), BF16),
-            pltpu.VMEM((sp - 1, depth, 9 * mid), BF16),
             pltpu.VMEM((sp - 1, mid, width), BF16),
             dma((dp - 1,)), dma((dp - 1,)), dma((dp - 1,)), dma((dp - 1,)),
             dma((dp - 1,)), dma((dp - 1,)), dma((dp - 1,)), dma((dp - 1,)),
             dma((sp - 1,)), dma((sp - 1,)), dma((4,)), dma((4,)),
-            dma((3, sp - 1)), dma((3, sp - 1)),
+            dma((4, sp - 1)), dma((4, sp - 1)), dma((5,)),
         ],
         compiler_params=pltpu.CompilerParams(
             collective_id=0, has_side_effects=True, vmem_limit_bytes=48 * 1024 * 1024

time: 111 us -> 92.7 us (0.84)
  Pallas kernels: 100 us -> 82.1 us
    pallas_call x1, Pallas kernels: 100 us -> 82.1 us  [body(): pl.pallas_call(functools.partial(kernel, (dp, sp, rows, cols, elems)), ou...]
where the time goes in v2:
time: 92.7 us; the launch traced here: 92.4 us
  Pallas kernels  82.1 us (89%)
  local copies, waits for them, and re-layouts  8.39 us (9%)
  between operations  1.82 us (2%)
    pallas_call x1, Pallas kernels, body(): pl.pallas_call(functools.partial(kernel, (dp, sp, rows, cols, elems)), ou...  82.1 us
    unnamed x14, local copies, waits for them, and re-layouts  8.39 us

profile of v2, /device:TPU:11, one launch (start us, length us, event | category | flops | bytes accessed | tf_op | source)
XLA Modules:
  0.0 92.4 jit_solution(7455219328155396828)
XLA Ops:
  0.6 0.0 copy-start
  0.6 1.2 %copy-done = bf16[1,4,128,1024]{3,2,1,0:T(8,128)(2,1)S(1)} copy-done((bf16[1,4,128,1024]{3,2,1,0:T(8,128)(2,1)S(1)}, bf16[1,4,128,1024]{3,2,1,0:T(8,128)(2,1)}, u32[]{:S(2)}) %copy-start) | copy-done | bytes 1048600
  1.9 0.0 copy-start.1
  1.9 1.2 %copy-done.1 = bf16[1,4,128,1024]{3,2,1,0:T(8,128)(2,1)S(1)} copy-done((bf16[1,4,128,1024]{3,2,1,0:T(8,128)(2,1)S(1)}, bf16[1,4,128,1024]{3,2,1,0:T(8,128)(2,1)}, u32[]{:S(2)}) %copy-start.1) | copy-done | bytes 1048600
  3.1 0.0 copy-start.2
  3.1 1.0 %copy-done.2 = bf16[1024,256]{1,0:T(8,128)(2,1)S(1)} copy-done((bf16[1024,256]{1,0:T(8,128)(2,1)S(1)}, bf16[1024,256]{1,0:T(8,128)(2,1)}, u32[]{:S(2)}) %copy-start.2) | copy-done | bytes 524312
  4.1 0.0 copy-start.3
  4.1 1.0 %copy-done.3 = bf16[256,1024]{1,0:T(8,128)(2,1)S(1)} copy-done((bf16[256,1024]{1,0:T(8,128)(2,1)S(1)}, bf16[256,1024]{1,0:T(8,128)(2,1)}, u32[]{:S(2)}) %copy-start.3) | copy-done | bytes 524312
  5.2 0.0 copy-start.4
  5.2 0.7 copy-done.4
  5.8 82.1 %distill.1 = (f32[1,128]{1,0:T(1,128)S(1)}, bf16[512,1024]{1,0:T(8,128)(2,1)S(1)}, f32[256,256]{1,0:T(8,128)S(1)}, f32[9,64,256]{2,1,0:T(8,128)S(1)}, f32[256,256]{1,0:T(8,128)S(1)}) custom-call(s32[2,8]{1,0:T(2,128)S(1)} %copy-done.4, bf16[512,1024]{1,0:T(8,128)(2,1)S(1)} %bitcast.11, bf16[512,1024]{1,0:T(8,128)(2,1)S(1)} %bitcast.12, ...), custom_call_target="tpu_custom_call" | custom-call | tf_op jit(solution)/shard_map/distill/pallas_call | solution.py:419
  88.0 1.0 %copy.17 = bf16[1,4,128,1024]{3,2,1,0:T(8,128)(2,1)} copy(bf16[1,4,128,1024]{3,2,1,0:T(8,128)(2,1)S(1)} %bitcast.13) | data formatting | bytes 2097152
  89.0 0.7 copy.18
  89.7 0.8 copy.19
  90.5 0.7 copy.20
Async XLA Ops:
  0.6 1.2 %copy-start = (bf16[1,4,128,1024]{3,2,1,0:T(8,128)(2,1)S(1)}, bf16[1,4,128,1024]{3,2,1,0:T(8,128)(2,1)}, u32[]{:S(2)}) copy-start(bf16[1,4,128,1024]{3,2,1,0:T(8,128)(2,1)} %param.6) | copy-start | bytes 3145732
  1.9 1.2 %copy-start.1 = (bf16[1,4,128,1024]{3,2,1,0:T(8,128)(2,1)S(1)}, bf16[1,4,128,1024]{3,2,1,0:T(8,128)(2,1)}, u32[]{:S(2)}) copy-start(bf16[1,4,128,1024]{3,2,1,0:T(8,128)(2,1)} %param.7) | copy-start | bytes 3145732
  3.1 1.0 %copy-start.2 = (bf16[1024,256]{1,0:T(8,128)(2,1)S(1)}, bf16[1024,256]{1,0:T(8,128)(2,1)}, u32[]{:S(2)}) copy-start(bf16[1024,256]{1,0:T(8,128)(2,1)} %wr_hbm.1) | copy-start | bytes 1572868
  4.1 1.0 %copy-start.3 = (bf16[256,1024]{1,0:T(8,128)(2,1)S(1)}, bf16[256,1024]{1,0:T(8,128)(2,1)}, u32[]{:S(2)}) copy-start(bf16[256,1024]{1,0:T(8,128)(2,1)} %we_hbm.1) | copy-start | bytes 1572868
  5.2 0.7 copy-start.4

commit v3 on v2

--- a/solution.py
+++ b/solution.py
@@ -466,7 +466,7 @@
             dma((4, sp - 1)), dma((4, sp - 1)), dma((5,)),
         ],
         compiler_params=pltpu.CompilerParams(
-            collective_id=0, has_side_effects=True, vmem_limit_bytes=48 * 1024 * 1024
+            collective_id=0, has_side_effects=True, vmem_limit_bytes=60 * 1024 * 1024
         ),
         name="distill",
     )(

time: 92.7 us -> 90.8 us (0.980)
  local copies, waits for them, and re-layouts: 8.39 us -> 4.56 us
  Pallas kernels: 82.1 us -> 83.6 us
    unnamed x14 -> x10, local copies, waits for them, and re-layouts: 8.39 us -> 4.56 us
    pallas_call x1, Pallas kernels: 82.1 us -> 83.6 us  [body(): pl.pallas_call(functools.partial(kernel, (dp, sp, rows, cols, elems)), ou...]
where the time goes in v3:
time: 90.8 us; the launch traced here: 90.7 us
  Pallas kernels  83.6 us (92%)
  local copies, waits for them, and re-layouts  4.56 us (5%)
  between operations  2.51 us (3%)
    pallas_call x1, Pallas kernels, body(): pl.pallas_call(functools.partial(kernel, (dp, sp, rows, cols, elems)), ou...  83.6 us
    unnamed x10, local copies, waits for them, and re-layouts  4.56 us

profile of v3, /device:TPU:11, one launch (start us, length us, event | category | flops | bytes accessed | tf_op | source)
XLA Modules:
  0.0 90.7 jit_solution(11701500415248738747)
XLA Ops:
  0.6 83.6 %distill.1 = (f32[1,128]{1,0:T(1,128)}, bf16[512,1024]{1,0:T(8,128)(2,1)}, f32[256,256]{1,0:T(8,128)}, f32[9,64,256]{2,1,0:T(8,128)}, f32[256,256]{1,0:T(8,128)}) custom-call(s32[2,8]{1,0:T(2,128)} %part.1, bf16[512,1024]{1,0:T(8,128)(2,1)} %bitcast.12, bf16[512,1024]{1,0:T(8,128)(2,1)} %bitcast.13, bf16[1024,256]{1,0:T(8,128)(2,1)} %wr_hbm.1, ...), custom_call_target="tpu_custom_call" | custom-call | tf_op jit(solution)/shard_map/distill/pallas_call | solution.py:419
  84.2 0.0 copy-start.2
  85.0 0.0 copy-start
  85.0 2.3 %copy.17 = bf16[1,4,128,1024]{3,2,1,0:T(8,128)(2,1)} copy(bf16[1,4,128,1024]{3,2,1,0:T(8,128)(2,1)} %bitcast.14) | data formatting | bytes 2097152
  87.3 0.0 copy-done.2
  87.3 0.0 copy-start.1
  87.3 0.7 copy.18
  88.0 0.0 copy-done
  88.0 0.8 copy.19
  88.8 0.0 copy-done.1
  88.8 0.7 copy.20
Async XLA Ops:
  84.2 3.1 %copy-start.2 = (f32[256,256]{1,0:T(8,128)S(1)}, f32[256,256]{1,0:T(8,128)}, u32[]{:S(2)}) copy-start(f32[256,256]{1,0:T(8,128)} %get-tuple-element.12) | copy-start | bytes 786436
  85.0 3.0 %copy-start = (f32[9,64,256]{2,1,0:T(8,128)S(1)}, f32[9,64,256]{2,1,0:T(8,128)}, u32[]{:S(2)}) copy-start(f32[9,64,256]{2,1,0:T(8,128)} %get-tuple-element.13) | copy-start | bytes 1769476
  87.3 1.5 %copy-start.1 = (f32[256,256]{1,0:T(8,128)S(1)}, f32[256,256]{1,0:T(8,128)}, u32[]{:S(2)}) copy-start(f32[256,256]{1,0:T(8,128)} %get-tuple-element.14) | copy-start | bytes 786436
